TPU v7x, 128 devices: a whole 4x4x4 slice. The times are simulated.
128 devices in a mesh: chan: 16 (over x, z_lo, core), beam: 8 (over z_hi, y).
Axes of the slice: x: 4, y: 4, z: 4 (z_hi: 2, z_lo: 2; z = z_hi * 2 + z_lo), core: 2. Of those that a mesh axis runs over, the one named last changes fastest.
Arguments:
- voltages: bfloat16 [512, 2048, 128], P(('chan', 'beam')), may hold values from -6 to 6
- station_map: int32 [512], replicated, may hold values from 0 to 511, each once
- delay: float32 [512, 512], replicated, may hold values from -2 to 2
- screen: float32 [64, 512], replicated, may hold values from -3 to 3
- beam_patch: int32 [512], replicated, may hold values from 0 to 63
Outputs:
- stokes: bfloat16 [512, 32, 2048], P(('beam', 'chan'))
Inputs may be any that keep to these rules, and one draw needn't show every extreme that they name: `station_map`: every station appears in exactly one slot.
All inputs are finite; a program needn't handle non-finite values.
Results may differ from a plain program's by a relative error of at most 0.0045.
Values may be sent and summed in bfloat16 or wider, within the bound.
A program may use at most 64 MiB of HBM per device.

v0:
```python
import math

import jax
import jax.numpy as jnp
import numpy as np
from jax import lax
from jax.experimental import pallas as pl
from jax.experimental.pallas import tpu as pltpu
from jax.sharding import PartitionSpec as P

F32, BF16 = jnp.float32, jnp.bfloat16
LOGICAL = pl.DeviceIdType.LOGICAL
STEP = 300.0 / 2048
DEVICES = 128
CHANS = 16
LANES = 128
CHUNKS = 4
PER_CHUNK = DEVICES // CHUNKS
GROUPS = 2
UNROLL = 8
STEPS = 4
EMIT_AT = CHUNKS - 1
PART = CHANS // GROUPS
WIDE = 256 // PART


def hops(offset):
    return sum(min(a, 4 - a) for a in offset[:3])


def route():
    lines = [(0, 0, 0)] + [tuple(d * (axis == i) for i in range(3)) for d in (2, 1, 3) for axis in range(3)]
    planes, rest = [], []
    for i in range(9):
        u, v = i % 3 + 1, (i + i // 3) % 3 + 1
        planes += [(u, v, 0), (0, u, v), (v, 0, u)]
    for i in range(27):
        rest.append((i % 3 + 1, (i + i // 3) % 3 + 1, (i + i // 9) % 3 + 1))
    every = [chip + (core,) for chip in lines + planes + rest for core in (1, 0)]
    own = (0, 0, 0, 0)
    return [o for o in every if o != own] + [own]


LINES, PLANES = 19, 54
ROUTE = route()
OUT_ROUTE = sorted(ROUTE, key=lambda o: -hops(o))


def position():
    chan, beam = lax.axis_index("chan"), lax.axis_index("beam")
    return chan // 4, beam % 4, (beam // 4) * 2 + (chan // 2) % 2, chan % 2


def places():
    x, y, z, c = position()
    xs = [(x + d) % 4 for d in range(4)]
    ys = [(y + d) % 4 for d in range(4)]
    zs = [(z + d) % 4 for d in range(4)]
    cs = [(c + d) % 2 for d in range(2)]
    index = ([v * 32 for v in xs], ys, [(v % 2) * 16 + (v // 2) * 4 for v in zs], [v * 8 for v in cs])
    owner = ([v * 4 for v in xs], [v * 16 for v in ys], [(v % 2) * 2 + (v // 2) * 64 for v in zs], cs)
    return index, owner


def at(shares, offset):
    return shares[0][offset[0]] + shares[1][offset[1]] + shares[2][offset[2]] + shares[3][offset[3]]


def fit(fn, odd, terms):
    nodes = (np.cos((2 * np.arange(400) + 1) * np.pi / 800) + 1) / 8
    r = np.sqrt(nodes)
    want = fn(2 * np.pi * r) / (r if odd else 1.0)
    cheb = np.polynomial.chebyshev.Chebyshev.fit(nodes, want, terms - 1, domain=[0, 0.25])
    return [float(v) for v in cheb.convert(kind=np.polynomial.Polynomial).coef]


SIN, COS = fit(np.sin, True, 7), fit(np.cos, False, 8)


def poly(coefs, z):
    total = jnp.full_like(z, coefs[-1])
    for value in coefs[-2::-1]:
        total = total * z + value
    return total


def turn(t):
    r = t - jnp.round(t)
    z = r * r
    return poly(COS, z), r * poly(SIN, z)


def split3(v):
    high = v.astype(BF16)
    rest = v - high.astype(F32)
    mid = rest.astype(BF16)
    low = (rest - mid.astype(F32)).astype(BF16)
    return high, mid, low


def pick(parts, hot, dims):
    total = None
    for part in parts:
        args = (hot, part) if dims == "left" else (part, hot)
        contract = (((0,), (0,)), ((), ())) if dims == "left" else (((1,), (0,)), ((), ()))
        term = lax.dot_general(*args, contract, preferred_element_type=F32)
        total = term if total is None else total + term
    return total


def kernel(
    volt, station_map, delay, screen, beam_patch, offsets, back,
    got, mine_in, delay_in, screen_in, map_in, patch_in, offs_in, delay_at, screen_at, bend, weights, vperm, acc, power,
    sent, load_sem, volt_send, volt_recv, own_sem, lines_in, planes_in, out_send, out_recv,
):
    index, owner = places()
    me = at(index, (0, 0, 0, 0))
    x, y, z, c = position()

    loads = [
        pltpu.make_async_copy(src, dst, load_sem.at[i])
        for i, (src, dst) in enumerate(
            [(station_map, map_in), (offsets, offs_in), (delay, delay_in), (screen, screen_in), (beam_patch, patch_in)]
        )
    ]
    for load in loads:
        load.start()
    barrier = pltpu.get_barrier_semaphore()
    for offset in ROUTE[:LINES]:
        pl.semaphore_signal(barrier, inc=1, device_id=at(index, offset), device_id_type=LOGICAL)
    own = pltpu.make_async_copy(volt.at[:, pl.ds(me * GROUPS, GROUPS), :, :], mine_in, own_sem)
    own.start()
    pl.semaphore_wait(barrier, LINES)

    def send(group, first, last):
        for k, offset in enumerate(ROUTE):
            if not first <= k < last:
                continue
            to = at(index, offset)
            pltpu.make_async_remote_copy(
                src_ref=volt.at[:, to * GROUPS + group, :, :],
                dst_ref=got.at[group, k],
                send_sem=volt_send.at[group],
                recv_sem=volt_recv.at[group, k // PER_CHUNK],
                device_id=to,
                device_id_type=LOGICAL,
            ).start()

    for d in (2, 1, 3):
        for offset in ((d, 0, 0, 0), (0, d, 0, 0)):
            pl.semaphore_signal(lines_in, inc=1, device_id=at(index, offset), device_id_type=LOGICAL)
    send(0, 0, LINES)
    pl.semaphore_wait(lines_in, 6)
    for d in (2, 1, 3):
        pl.semaphore_signal(planes_in, inc=1, device_id=at(index, (d, 0, 0, 0)), device_id_type=LOGICAL)
    send(0, LINES, LINES + PLANES)
    for load in loads:
        load.wait()

    col = lax.broadcasted_iota(jnp.int32, (1, 512), 1)
    sx = jnp.bitwise_and(x - offs_in[0:1, :], 3)
    sy = jnp.bitwise_and(y - offs_in[1:2, :], 3)
    sz = jnp.bitwise_and(z - offs_in[2:3, :], 3)
    sc = jnp.bitwise_and(c - offs_in[3:4, :], 1)
    slot = (sx * 32 + sy + jnp.bitwise_and(sz, 1) * 16 + jnp.right_shift(sz, 1) * 4 + sc * 8) * 4
    slot = slot + jnp.bitwise_and(col, 3)
    rows = lax.broadcasted_iota(jnp.int32, (512, 512), 0)
    order = (rows == slot).astype(F32).astype(BF16)
    names = map_in[...].reshape(1, 512)
    tops = jnp.right_shift(names, 4).astype(F32).astype(BF16)
    lows = jnp.bitwise_and(names, 15).astype(F32).astype(BF16)
    halves = jnp.dot(
        jnp.concatenate([jnp.broadcast_to(tops, (16, 512)), jnp.broadcast_to(lows, (16, 512))], axis=0),
        order,
        preferred_element_type=F32,
    )
    station = (halves[0:1] * 16.0 + halves[16:17]).astype(jnp.int32)
    hot = (rows == station).astype(F32).astype(BF16)
    ordered = pick(split3(delay_in[...]), hot, "right")
    for chunk in range(CHUNKS):
        delay_at[chunk] = ordered[:, chunk * LANES : (chunk + 1) * LANES]
    patches = (
        lax.broadcasted_iota(jnp.int32, (64, 512), 0) == patch_in[...].reshape(1, 512)
    ).astype(F32).astype(BF16)
    ordered = pick(split3(pick(split3(screen_in[...]), hot, "right")), patches, "left")
    for chunk in range(CHUNKS):
        screen_at[chunk] = ordered[:, chunk * LANES : (chunk + 1) * LANES]

    pl.semaphore_wait(planes_in, 3)
    send(0, LINES + PLANES, DEVICES - 1)
    send(1, 0, DEVICES - 1)

    first = (lax.broadcasted_iota(jnp.int32, (8, LANES), 0) * 0 + me * CHANS).astype(F32)

    def freq(k):
        return 50.0 + (first + (k + 0.5)) * STEP

    for k in range(CHANS - 2):
        bend[k] = (2.0 * 150.0 * STEP * STEP) / (freq(k) * freq(k + 1) * freq(k + 2))
    tau = 2.0 * math.pi
    scale = 1.0 / math.sqrt(512.0)
    high = 32

    def fill(i, _):
        chunk = i // 16
        block = i % 16
        j = block // 4
        start = j + 4 * high * (block % 4)
        d = delay_at[chunk, pl.ds(start, high, stride=4), :]
        s = screen_at[chunk, pl.ds(start, high, stride=4), :]
        f0, f1 = freq(0)[0:1], freq(1)[0:1]
        c0, s0 = turn(f0 * d + s * ((150.0 / tau) / f0))
        rc, rs = turn(STEP * d - s * ((150.0 / tau) * STEP / (f0 * f1)))
        wr, wi = c0 * scale, s0 * scale
        here = pl.ds(pl.multiple_of(block * high, high), high)
        for k in range(CHANS):
            weights[k, chunk, here, 0:LANES] = wr.astype(BF16)
            weights[k, chunk, here, LANES : 2 * LANES] = wi.astype(BF16)
            if k < CHANS - 1:
                wr, wi = wr * rc - wi * rs, wr * rs + wi * rc
            if k < CHANS - 2:
                turned = s * bend[k, 0:1, :]
                rc, rs = rc - turned * rs, rs + turned * rc
        return 0

    lax.fori_loop(0, 16 * CHUNKS, fill, 0)

    r = lax.broadcasted_iota(jnp.int32, (256, 256), 0)
    q = lax.broadcasted_iota(jnp.int32, (256, 256), 1)
    apart = (r == (q % PART) * WIDE + q // PART).astype(F32).astype(BF16)
    together = (q == (r % PART) * WIDE + r // PART).astype(F32).astype(BF16)
    lane = lax.broadcasted_iota(jnp.int32, (1, LANES), 1)
    low_half = lane < 64
    even = jnp.bitwise_and(lane, 32) == 0
    own.wait()

    def emit(group):
        for offset in OUT_ROUTE[:-1]:
            pltpu.make_async_remote_copy(
                src_ref=sent.at[group, at(owner, offset)],
                dst_ref=back.at[me, group],
                send_sem=out_send.at[group],
                recv_sem=out_recv,
                device_id=at(index, offset),
                device_id_type=LOGICAL,
            ).start()
        keep = pltpu.make_async_copy(sent.at[group, at(owner, (0, 0, 0, 0))], back.at[me, group], own_sem)
        keep.start()
        keep.wait()

    for group in range(GROUPS):
        got[group, DEVICES - 1] = mine_in[:, group]
        for chunk in range(CHUNKS):
            if group and chunk == EMIT_AT:
                emit(group - 1)
            n = PER_CHUNK - (1 if chunk == CHUNKS - 1 else 0)
            landed = got.at[group, pl.ds(chunk * PER_CHUNK, n)]
            pltpu.make_async_copy(landed, landed, volt_recv.at[group, chunk]).wait()
            srcs = WIDE // 4
            for m in range(PER_CHUNK // srcs):
                block = got[group, pl.ds(chunk * PER_CHUNK + srcs * m, srcs)].reshape(256, LANES)
                turned = jnp.dot(apart, block, preferred_element_type=F32)
                other = pltpu.roll(turned, 64, 1)
                other = jnp.where(low_half, other, -other)
                here = WIDE * m
                vperm[:, here : here + WIDE, :] = turned.astype(BF16).reshape(PART, WIDE, LANES)
                vperm[:, LANES + here : LANES + here + WIDE, :] = other.astype(BF16).reshape(PART, WIDE, LANES)

            def beams(step, _):
                for u in range(UNROLL):
                    k = step * UNROLL + u
                    part = jnp.dot(weights[group * PART + k, chunk], vperm[k], preferred_element_type=F32)
                    if chunk == 0:
                        acc[k] = part
                    elif chunk < CHUNKS - 1:
                        acc[k] += part
                    else:
                        total = acc[k] + part
                        sq = (total * total).reshape(4, LANES, LANES)
                        one = jnp.where(low_half, sq[0], sq[2])
                        one += pltpu.roll(jnp.where(low_half, sq[2], sq[0]), 64, 1)
                        two = jnp.where(low_half, sq[1], sq[3])
                        two += pltpu.roll(jnp.where(low_half, sq[3], sq[1]), 64, 1)
                        both = jnp.where(even, one, two)
                        both += jnp.where(even, pltpu.roll(one, 96, 1), pltpu.roll(two, 32, 1))
                        power[k] = (0.25 * both).astype(BF16)
                return 0

            lax.fori_loop(0, PART // UNROLL, beams, 0)

        for m in range(DEVICES // WIDE):
            block = power[:, WIDE * m : WIDE * m + WIDE, :].reshape(256, LANES)
            sent[group, WIDE * m : WIDE * m + WIDE] = (
                jnp.dot(together, block, preferred_element_type=F32).astype(BF16).reshape(WIDE, PART, LANES)
            )
        if group == GROUPS - 1:
            emit(group)

    rest = back.at[pl.ds(0, DEVICES - 1)]
    pltpu.make_async_copy(rest, rest, out_recv).wait()
    for group in range(GROUPS):
        gone = got.at[group, pl.ds(0, DEVICES - 1)]
        pltpu.make_async_copy(gone, gone, volt_send.at[group]).wait()
        gone = sent.at[group, pl.ds(0, DEVICES - 1)]
        pltpu.make_async_copy(gone, gone, out_send.at[group]).wait()


def transpose(rows, out, turned, sems):
    eye = (
        lax.broadcasted_iota(jnp.int32, (LANES, LANES), 0) == lax.broadcasted_iota(jnp.int32, (LANES, LANES), 1)
    ).astype(F32).astype(BF16)
    count = DEVICES * CHANS // STEPS
    copies = []
    for i in range(STEPS):
        block = rows[pl.ds(i * DEVICES // STEPS, DEVICES // STEPS)].reshape(count, LANES)
        final = lax.dot_general(eye, block, (((1,), (1,)), ((), ())), preferred_element_type=F32)
        turned[i] = final.astype(BF16).reshape(4, 32, count)
        copy = pltpu.make_async_copy(turned.at[i], out.at[:, :, pl.ds(i * count, count)], sems.at[i])
        copy.start()
        copies.append(copy)
    for copy in copies:
        copy.wait()


def body(voltages, station_map, delay, screen, beam_patch):
    table = np.zeros((8, 512), np.int32)
    for k, offset in enumerate(ROUTE):
        table[:4, 4 * k : 4 * k + 4] = np.array(offset, np.int32)[:, None]
    anywhere = pl.BlockSpec(memory_space=pl.ANY)
    power = pl.pallas_call(
        kernel,
        out_shape=pltpu.VMEM((DEVICES, GROUPS, PART, LANES), BF16),
        in_specs=[anywhere] * 6,
        out_specs=anywhere,
        scratch_shapes=[
            pltpu.VMEM((GROUPS, DEVICES, 4, PART, LANES), BF16),
            pltpu.VMEM((4, GROUPS, PART, LANES), BF16),
            pltpu.VMEM((512, 512), F32),
            pltpu.VMEM((64, 512), F32),
            pltpu.VMEM((512,), jnp.int32),
            pltpu.VMEM((512,), jnp.int32),
            pltpu.VMEM((8, 512), jnp.int32),
            pltpu.VMEM((CHUNKS, 512, LANES), F32),
            pltpu.VMEM((CHUNKS, 512, LANES), F32),
            pltpu.VMEM((CHANS, 8, LANES), F32),
            pltpu.VMEM((CHANS, CHUNKS, 512, 2 * LANES), BF16),
            pltpu.VMEM((PART, 2 * LANES, LANES), BF16),
            pltpu.VMEM((PART, 512, LANES), F32),
            pltpu.VMEM((PART, LANES, LANES), BF16),
            pltpu.VMEM((GROUPS, DEVICES, PART, LANES), BF16),
            pltpu.SemaphoreType.DMA((5,)),
            pltpu.SemaphoreType.DMA((GROUPS,)),
            pltpu.SemaphoreType.DMA((GROUPS, CHUNKS)),
            pltpu.SemaphoreType.DMA,
            pltpu.SemaphoreType.REGULAR,
            pltpu.SemaphoreType.REGULAR,
            pltpu.SemaphoreType.DMA((GROUPS,)),
            pltpu.SemaphoreType.DMA,
        ],
        compiler_params=pltpu.CompilerParams(collective_id=0, has_side_effects=True, vmem_limit_bytes=56 * 2**20),
        name="beamform",
    )(voltages.reshape(4, DEVICES * GROUPS, PART, LANES), station_map, delay, screen, beam_patch, jnp.asarray(table))
    return pl.pallas_call(
        transpose,
        out_shape=jax.ShapeDtypeStruct((4, 32, DEVICES * CHANS), BF16),
        in_specs=[pl.BlockSpec(memory_space=pltpu.VMEM)],
        out_specs=anywhere,
        scratch_shapes=[
            pltpu.VMEM((STEPS, 4, 32, DEVICES * CHANS // STEPS), BF16),
            pltpu.SemaphoreType.DMA((STEPS,)),
        ],
        name="transpose",
    )(pltpu.with_memory_space_constraint(power, pltpu.VMEM))


def solution(mesh):
    placed = (P(("chan", "beam"), None, None), P(), P(), P(), P())
    return jax.shard_map(
        body, mesh=mesh, in_specs=placed, out_specs=P(("beam", "chan"), None, None), check_vma=False
    )
```

profile of v0, /device:TPU:1, one launch (start us, length us, event | category | flops | bytes accessed | tf_op | source)
XLA Modules:
  0.0 45.2 jit_solution(1618592943143119220)
XLA Ops:
  0.0 44.0 %beamform.1.rows = bf16[128,2,8,128]{3,2,1,0:T(8,128)(2,1)S(1)} custom-call(bf16[4,256,8,128]{3,2,1,0:T(8,128)(2,1)} %bitcast.1, s32[512]{0:T(512)} %station_map.1, f32[512,512]{1,0:T(8,128)} %delay.1, f32[64,512]{1,0:T(8,128)} %screen.1, s32[512]{0:T(512)} %beam_patch.1, s32[8,512]{1,0:T(8,128)} %constant.2.clone.offsets), custom_call_target="tpu_custom_call" | custom-call | tf_op jit(solution)/shard_map/beamform/pallas_call | solution.py:330
  44.0 1.0 %transpose.1 = bf16[4,32,2048]{2,1,0:T(8,128)(2,1)} custom-call(bf16[128,2,8,128]{3,2,1,0:T(8,128)(2,1)S(1)} %beamform.1.rows), custom_call_target="tpu_custom_call" | custom-call | tf_op jit(solution)/shard_map/transpose/pallas_call | solution.py:363
where the time goes:
time: 45.3 us; the launch traced here: 45.2 us
  Pallas kernels  45.1 us (100%)
    pallas_call x1, Pallas kernels, body(): pl.pallas_call(kernel, out_shape=pltpu.VMEM((DEVICES, GROUPS, PART, LANES...  44 us
    pallas_call x1, Pallas kernels, body(): pl.pallas_call(transpose, out_shape=jax.ShapeDtypeStruct((4, 32, DEVICES...  1.02 us

commit v1 on v0

--- a/solution.py
+++ b/solution.py
@@ -111,12 +111,15 @@
 def kernel(
     volt, station_map, delay, screen, beam_patch, offsets, back,
     got, mine_in, delay_in, screen_in, map_in, patch_in, offs_in, delay_at, screen_at, bend, weights, vperm, acc, power,
-    sent, load_sem, volt_send, volt_recv, own_sem, lines_in, planes_in, out_send, out_recv,
+    sent, load_sem, volt_send, volt_recv, own_sem, keep_sem, lines_in, planes_in, out_send, out_recv,
 ):
     index, owner = places()
     me = at(index, (0, 0, 0, 0))
     x, y, z, c = position()
 
+    barrier = pltpu.get_barrier_semaphore()
+    for offset in ROUTE[:LINES]:
+        pl.semaphore_signal(barrier, inc=1, device_id=at(index, offset), device_id_type=LOGICAL)
     loads = [
         pltpu.make_async_copy(src, dst, load_sem.at[i])
         for i, (src, dst) in enumerate(
@@ -125,9 +128,6 @@
     ]
     for load in loads:
         load.start()
-    barrier = pltpu.get_barrier_semaphore()
-    for offset in ROUTE[:LINES]:
-        pl.semaphore_signal(barrier, inc=1, device_id=at(index, offset), device_id_type=LOGICAL)
     own = pltpu.make_async_copy(volt.at[:, pl.ds(me * GROUPS, GROUPS), :, :], mine_in, own_sem)
     own.start()
     pl.semaphore_wait(barrier, LINES)
@@ -234,6 +234,8 @@
     even = jnp.bitwise_and(lane, 32) == 0
     own.wait()
 
+    kept = []
+
     def emit(group):
         for offset in OUT_ROUTE[:-1]:
             pltpu.make_async_remote_copy(
@@ -244,9 +246,9 @@
                 device_id=at(index, offset),
                 device_id_type=LOGICAL,
             ).start()
-        keep = pltpu.make_async_copy(sent.at[group, at(owner, (0, 0, 0, 0))], back.at[me, group], own_sem)
+        keep = pltpu.make_async_copy(sent.at[group, at(owner, (0, 0, 0, 0))], back.at[me, group], keep_sem.at[group])
         keep.start()
-        keep.wait()
+        kept.append(keep)
 
     for group in range(GROUPS):
         got[group, DEVICES - 1] = mine_in[:, group]
@@ -296,6 +298,8 @@
         if group == GROUPS - 1:
             emit(group)
 
+    for keep in kept:
+        keep.wait()
     rest = back.at[pl.ds(0, DEVICES - 1)]
     pltpu.make_async_copy(rest, rest, out_recv).wait()
     for group in range(GROUPS):
@@ -352,6 +356,7 @@
             pltpu.SemaphoreType.DMA((GROUPS,)),
             pltpu.SemaphoreType.DMA((GROUPS, CHUNKS)),
             pltpu.SemaphoreType.DMA,
+            pltpu.SemaphoreType.DMA((GROUPS,)),
             pltpu.SemaphoreType.REGULAR,
             pltpu.SemaphoreType.REGULAR,
             pltpu.SemaphoreType.DMA((GROUPS,)),

time: 45.3 us -> 45.3 us (level)
  no operation moved by 1% of the time
where the time goes in v1:
time: 45.3 us; the launch traced here: 45.2 us
  Pallas kernels  45.1 us (100%)
    pallas_call x1, Pallas kernels, body(): pl.pallas_call(kernel, out_shape=pltpu.VMEM((DEVICES, GROUPS, PART, LANES...  44 us
    pallas_call x1, Pallas kernels, body(): pl.pallas_call(transpose, out_shape=jax.ShapeDtypeStruct((4, 32, DEVICES...  1.02 us

profile of v1, /device:TPU:1, one launch (start us, length us, event | category | flops | bytes accessed | tf_op | source)
XLA Modules:
  0.0 45.2 jit_solution(14549521847994390442)
XLA Ops:
  0.0 44.0 %beamform.1.rows = bf16[128,2,8,128]{3,2,1,0:T(8,128)(2,1)S(1)} custom-call(bf16[4,256,8,128]{3,2,1,0:T(8,128)(2,1)} %bitcast.1, s32[512]{0:T(512)} %station_map.1, f32[512,512]{1,0:T(8,128)} %delay.1, f32[64,512]{1,0:T(8,128)} %screen.1, s32[512]{0:T(512)} %beam_patch.1, s32[8,512]{1,0:T(8,128)} %constant.2.clone.offsets), custom_call_target="tpu_custom_call" | custom-call | tf_op jit(solution)/shard_map/beamform/pallas_call | solution.py:334
  44.1 1.0 %transpose.1 = bf16[4,32,2048]{2,1,0:T(8,128)(2,1)} custom-call(bf16[128,2,8,128]{3,2,1,0:T(8,128)(2,1)S(1)} %beamform.1.rows), custom_call_target="tpu_custom_call" | custom-call | tf_op jit(solution)/shard_map/transpose/pallas_call | solution.py:368

commit v2 on v0

--- a/solution.py
+++ b/solution.py
@@ -16,6 +16,7 @@
 LANES = 128
 CHUNKS = 4
 PER_CHUNK = DEVICES // CHUNKS
+PER_WAIT = PER_CHUNK // 2
 GROUPS = 2
 UNROLL = 8
 STEPS = 4
@@ -141,7 +142,7 @@
                 src_ref=volt.at[:, to * GROUPS + group, :, :],
                 dst_ref=got.at[group, k],
                 send_sem=volt_send.at[group],
-                recv_sem=volt_recv.at[group, k // PER_CHUNK],
+                recv_sem=volt_recv.at[group, k // PER_WAIT],
                 device_id=to,
                 device_id_type=LOGICAL,
             ).start()
@@ -253,11 +254,12 @@
         for chunk in range(CHUNKS):
             if group and chunk == EMIT_AT:
                 emit(group - 1)
-            n = PER_CHUNK - (1 if chunk == CHUNKS - 1 else 0)
-            landed = got.at[group, pl.ds(chunk * PER_CHUNK, n)]
-            pltpu.make_async_copy(landed, landed, volt_recv.at[group, chunk]).wait()
             srcs = WIDE // 4
             for m in range(PER_CHUNK // srcs):
+                first = chunk * PER_CHUNK + srcs * m
+                if first % PER_WAIT == 0:
+                    landed = got.at[group, pl.ds(first, min(PER_WAIT, DEVICES - 1 - first))]
+                    pltpu.make_async_copy(landed, landed, volt_recv.at[group, first // PER_WAIT]).wait()
                 block = got[group, pl.ds(chunk * PER_CHUNK + srcs * m, srcs)].reshape(256, LANES)
                 turned = jnp.dot(apart, block, preferred_element_type=F32)
                 other = pltpu.roll(turned, 64, 1)
@@ -350,7 +352,7 @@
             pltpu.VMEM((GROUPS, DEVICES, PART, LANES), BF16),
             pltpu.SemaphoreType.DMA((5,)),
             pltpu.SemaphoreType.DMA((GROUPS,)),
-            pltpu.SemaphoreType.DMA((GROUPS, CHUNKS)),
+            pltpu.SemaphoreType.DMA((GROUPS, DEVICES // PER_WAIT)),
             pltpu.SemaphoreType.DMA,
             pltpu.SemaphoreType.REGULAR,
             pltpu.SemaphoreType.REGULAR,

time: 45.3 us -> 45.3 us (level)
  no operation moved by 1% of the time
where the time goes in v2:
time: 45.3 us; the launch traced here: 45.2 us
  Pallas kernels  45 us (99%)
    pallas_call x1, Pallas kernels, body(): pl.pallas_call(kernel, out_shape=pltpu.VMEM((DEVICES, GROUPS, PART, LANES...  44 us
    pallas_call x1, Pallas kernels, body(): pl.pallas_call(transpose, out_shape=jax.ShapeDtypeStruct((4, 32, DEVICES...  1.01 us

profile of v2, /device:TPU:1, one launch (start us, length us, event | category | flops | bytes accessed | tf_op | source)
XLA Modules:
  0.0 45.2 jit_solution(1869519149939849294)
XLA Ops:
  0.0 44.0 %beamform.1.rows = bf16[128,2,8,128]{3,2,1,0:T(8,128)(2,1)S(1)} custom-call(bf16[4,256,8,128]{3,2,1,0:T(8,128)(2,1)} %bitcast.1, s32[512]{0:T(512)} %station_map.1, f32[512,512]{1,0:T(8,128)} %delay.1, f32[64,512]{1,0:T(8,128)} %screen.1, s32[512]{0:T(512)} %beam_patch.1, s32[8,512]{1,0:T(8,128)} %constant.2.clone.offsets), custom_call_target="tpu_custom_call" | custom-call | tf_op jit(solution)/shard_map/beamform/pallas_call | solution.py:332
  44.0 1.0 %transpose.1 = bf16[4,32,2048]{2,1,0:T(8,128)(2,1)} custom-call(bf16[128,2,8,128]{3,2,1,0:T(8,128)(2,1)S(1)} %beamform.1.rows), custom_call_target="tpu_custom_call" | custom-call | tf_op jit(solution)/shard_map/transpose/pallas_call | solution.py:365
